TPU v7x, 32 devices: a whole 2x2x4 slice. The times are simulated.
32 devices in a mesh: ta: 4 (over x, core), ha: 4 (over z), hd: 2 (over y).
Axes of the slice: x: 2, y: 2, z: 4, core: 2. Of those that a mesh axis runs over, the one named last changes fastest.
Arguments:
- qkv: bfloat16 [16, 16, 64, 9216], P('ta', 'ha', 'hd'), may hold values from -40 to 40, as said below
- q_gain: float32 [128], replicated, may hold values from 0.5 to 4.5
- k_gain: float32 [128], replicated, may hold values from 0.5 to 4.5
- windows: int32 [24, 3], P('hd'), may hold values from 0 to 1, as said below
- frame_counts: int32 [8], replicated, may hold values from 1 to 2, as said below
- row_counts: int32 [8], replicated, may hold values from 1 to 2, as said below
Outputs:
- attended: bfloat16 [16, 16, 64, 3072], P('ta', 'ha', 'hd')
Inputs may be any that keep to these rules, and one draw needn't show every extreme that they name: `qkv`: the last dimension holds the query, then the key, then the value, each as 24 heads of 128 entries. `windows`: every column reaches 1 for some head. `frame_counts`: some tile holds 2 frames. `row_counts`: some tile holds 2 rows.
All inputs are finite; a program needn't handle non-finite values.
Results may differ from a plain program's by a relative error of at most 0.012.
The roundings to bfloat16 on the way count: a program that leaves them out, or rounds other values in their place, can miss the bound.
Values may be sent and summed in bfloat16 or wider, within the bound.
A program may use at most 128 MiB of HBM per device.

v0:
```python
import math

import jax
import jax.numpy as jnp
from jax import lax
from jax.sharding import PartitionSpec as P

TT = 2
TH = 2
TW = 8


def extended(value, sides, width):
    for axis, dim in sides:
        size, length = (lax.axis_size(axis), value.shape[dim])
        up = [(i, (i + 1) % size) for i in range(size - 1)]
        down = [(j, i) for i, j in up]
        last = lax.slice_in_dim(value, length - width, length, axis=dim)
        initial = lax.slice_in_dim(value, 0, width, axis=dim)
        before = lax.ppermute(last, axis, up)
        after = lax.ppermute(initial, axis, down)
        value = jnp.concatenate([before, value, after], axis=dim)
    return value


def normalize(part_values, gain):
    widened = part_values.astype(jnp.float32)
    meansq = jnp.mean(widened * widened, axis=-1, keepdims=True)
    return (widened * lax.rsqrt(meansq + 1e-06) * gain).astype(jnp.bfloat16)


def valid_cells(position, extent, counts):
    tile_index = position // extent
    listed = jnp.arange(counts.shape[0], dtype=jnp.int32)
    holding = jnp.sum(jnp.where(tile_index[:, None] == listed[None, :], counts[None, :], 0), axis=1)
    return position % extent < holding


def extend_rims(paired):
    grown = extended(paired, (("ta", 0), ("ha", 1)), TT)
    return grown


def shards(qkv, q_gain, k_gain, windows, frame_counts, row_counts):
    frame_num, row_num, col_local, channels = qkv.shape
    head_dim = q_gain.shape[0]
    heads_all = channels // (3 * head_dim)
    sectioned = qkv.reshape(frame_num, row_num, col_local, 3, heads_all, head_dim)
    spread = lax.all_to_all(sectioned, "hd", split_axis=4, concat_axis=2, tiled=True)
    queries = normalize(spread[:, :, :, 0], q_gain)
    paired = jnp.stack([normalize(spread[:, :, :, 1], k_gain), spread[:, :, :, 2]], axis=3)
    padded = extend_rims(paired)
    col_num = queries.shape[2]
    heads_local = queries.shape[3]
    frame_base = lax.axis_index("ta") * frame_num
    row_base = lax.axis_index("ha") * row_num
    time_tiles = frame_num // TT
    score_scale = 1.0 / math.sqrt(head_dim)
    col_tiles = jnp.arange(col_num, dtype=jnp.int32) // TW
    col_gap = jnp.abs(col_tiles[:, None] - col_tiles[None, :])
    query_rows = row_base + jnp.arange(row_num, dtype=jnp.int32)
    key_rows = row_base - TH + jnp.arange(row_num + 2 * TH, dtype=jnp.int32)
    row_gap = jnp.abs(query_rows[:, None] // TH - key_rows[None, :] // TH)
    row_valid = valid_cells(key_rows, TH, row_counts)
    query_row_valid = valid_cells(query_rows, TH, row_counts)

    def attend(item_index):
        tile_at = item_index // heads_local
        head_at = item_index % heads_local
        first_frame = tile_at * TT
        query_block = lax.dynamic_slice(
            queries, (first_frame, 0, 0, head_at, 0), (TT, row_num, col_num, 1, head_dim)
        ).reshape(-1, head_dim)
        pair_block = lax.dynamic_slice(
            padded,
            (first_frame, 0, 0, 0, head_at, 0),
            (3 * TT, row_num + 2 * TH, col_num, 2, 1, head_dim),
        )
        key_block = pair_block[:, :, :, 0, 0].reshape(-1, head_dim)
        value_block = pair_block[:, :, :, 1, 0].reshape(-1, head_dim)
        radius = windows[head_at]
        query_frames = frame_base + first_frame + jnp.arange(TT, dtype=jnp.int32)
        key_frames = frame_base + first_frame - TT + jnp.arange(3 * TT, dtype=jnp.int32)
        time_mask = (
            jnp.abs(query_frames[:, None] // TT - key_frames[None, :] // TT) <= radius[0]
        ) & valid_cells(key_frames, TT, frame_counts)[None, :]
        row_mask = (row_gap <= radius[1]) & row_valid[None, :]
        col_mask = col_gap <= radius[2]
        allowed = (
            time_mask[:, None, None, :, None, None]
            & row_mask[None, :, None, None, :, None]
            & col_mask[None, None, :, None, None, :]
        ).reshape(query_block.shape[0], key_block.shape[0])
        query_live = (
            valid_cells(query_frames, TT, frame_counts)[:, None, None]
            & query_row_valid[None, :, None]
            & (col_tiles >= 0)[None, None, :]
        ).reshape(-1)
        scores = (
            jnp.einsum("qd,kd->qk", query_block, key_block, preferred_element_type=jnp.float32)
            * score_scale
        )
        scores = jnp.where(allowed, scores, -1e30)
        highest = jnp.max(scores, axis=1, keepdims=True)
        raised = jnp.exp(scores - highest)
        summed = jnp.sum(raised, axis=1, keepdims=True)
        weights = raised.astype(jnp.bfloat16)
        blended = jnp.dot(weights, value_block, preferred_element_type=jnp.float32)
        result = jnp.where(query_live[:, None], blended / summed, 0.0)
        return result.astype(jnp.bfloat16).reshape(TT, row_num, col_num, head_dim)

    outputs = lax.map(attend, jnp.arange(time_tiles * heads_local, dtype=jnp.int32))
    outputs = outputs.reshape(time_tiles, heads_local, TT, row_num, col_num, head_dim)
    outputs = outputs.transpose(0, 2, 3, 4, 1, 5).reshape(
        frame_num, row_num, col_num, heads_local, head_dim
    )
    gathered = lax.all_to_all(outputs, "hd", split_axis=2, concat_axis=3, tiled=True)
    return gathered.reshape(frame_num, row_num, col_local, heads_all * head_dim)


def solution(mesh):
    return jax.shard_map(
        shards,
        mesh=mesh,
        in_specs=(P("ta", "ha", "hd", None), P(), P(), P("hd", None), P(), P()),
        out_specs=P("ta", "ha", "hd", None),
        check_vma=False,
    )
```

profile of v0, /device:TPU:1, one launch (start us, length us, event | category | flops | bytes accessed | tf_op | source)
XLA Modules:
  0.0 1099.9 jit_solution(13470153321217038089)
XLA Ops:
  0.0 10.0 copy.46
  10.0 9.8 copy.32
  19.7 115.8 %all_to_all.33 = bf16[4,4,32,3,24,128]{5,2,3,1,0,4:T(8,128)(2,1)} all-to-all(bf16[4,4,32,3,24,128]{5,2,3,1,0,4:T(8,128)(2,1)} %copy.32), channel_id=1, replica_groups=mesh['ta'=4,'ha'=4,'hd'=2] {'hd'}, dimensions={4} | all-to-all | bytes 18874368 | tf_op jit(solution)/shard_map/all_to_all | solution.py:49
  135.6 10.3 copy.34
  145.9 3.6 fusion.25
  152.5 3.8 fusion.27
  163.6 33.4 %collective-permute-done.1 = bf16[2,4,64,2,12,128]{5,2,4,3,1,0:T(8,128)(2,1)S(1)} collective-permute-done((bf16[2,4,64,2,12,128]{5,2,4,3,1,0:T(8,128)(2,1)S(1)}, bf16[2,4,64,2,12,128]{5,2,4,3,1,0:T(8,128)(2,1)S(1)}, u32[]{:S(2)}, u32[]{:S(2)}) %collective-permute-start.1) | collective-permute-done | bytes 3145760 | tf_op jit(solution)/shard_map/ppermute | solution.py:21
  199.6 5.9 fusion.36
  206.8 6.7 collective-permute-start.2
  217.6 5.1 fusion.30
  222.7 92.9 %collective-permute-done.3 = bf16[8,2,64,2,12,128]{5,2,4,3,1,0:T(8,128)(2,1)} collective-permute-done((bf16[8,2,64,2,12,128]{5,2,4,3,1,0:T(8,128)(2,1)}, bf16[8,2,64,2,12,128]{5,2,4,3,1,0:T(8,128)(2,1)}, u32[]{:S(2)}, u32[]{:S(2)}) %collective-permute-start.3) | collective-permute-done | bytes 6291488 | tf_op jit(solution)/shard_map/ppermute | solution.py:21
  317.4 16.4 %pad_maximum_fusion = bf16[8,8,64,2,12,128]{5,2,4,3,1,0:T(8,128)(2,1)} fusion(bf16[8,2,64,2,12,128]{5,2,4,3,1,0:T(8,128)(2,1)} %collective-permute-done.3, bf16[2,4,64,2,12,128]{5,2,4,3,1,0:T(8,128)(2,1)} %copy-done.3, bf16[4,4,64,1,12,128]{5,2,4,3,1,0:T(8,128)(2,1)S(1)} %slice.73, bf16[4,4,64,1,12,128]{5,2,4,3,1,0:T(8,128)(2,1)} %copy-done.2, ...), kind=kLoop, calls=%fused_computation.48 | loop fusion | flops 62914560 | bytes 50331648 | tf_op jit(solution)/shard_map/concatenate | solution.py:22
  333.8 725.6 %while.14 = (s32[]{:T(128)}, bf16[24,2,4,64,128]{4,3,2,1,0:T(8,128)(2,1)}, s32[24]{0:T(128)S(1)}, s32[]{:T(128)}, s32[8]{0:T(128)S(1)}, /*index=5*/pred[4]{0:T(5...) while((s32[]{:T(128)}, ...), condition=%wide.region_9.10_spmd.clone, body=%wide.region_4.9_spmd.clone.sunk | while | flops 818099200 | bytes 59005084 | solution.py:112
  343.5 7.8 and.445
  359.5 3.8 fusion.65
  373.7 7.8 and.445
  389.8 3.8 fusion.65
  403.9 7.8 and.445
  420.0 3.8 fusion.65
  434.2 7.8 and.445
  450.2 3.8 fusion.65
  464.4 7.8 and.445
  480.5 3.8 fusion.65
  494.6 7.8 and.445
  510.7 3.8 fusion.65
  524.9 7.8 and.445
  540.9 3.8 fusion.65
  555.1 7.8 and.445
  571.2 3.8 fusion.65
  585.3 7.8 and.445
  601.4 3.8 fusion.65
  615.6 7.8 and.445
  631.6 3.8 fusion.65
  645.8 7.8 and.445
  661.9 3.8 fusion.65
  676.0 7.8 and.445
  692.1 3.8 fusion.65
  706.3 7.8 and.445
  722.3 3.8 fusion.65
  736.5 7.8 and.445
  752.5 3.8 fusion.65
  766.7 7.8 and.445
  782.8 3.8 fusion.65
  797.0 7.8 and.445
  813.0 3.8 fusion.65
  827.2 7.8 and.445
  843.2 3.8 fusion.65
  857.4 7.8 and.445
  873.5 3.8 fusion.65
  887.6 7.8 and.445
  903.7 3.8 fusion.65
  917.9 7.8 and.445
  933.9 3.8 fusion.65
  948.1 7.8 and.445
  964.2 3.8 fusion.65
  978.3 7.8 and.445
  994.4 3.8 fusion.65
  1008.6 7.8 and.445
  1024.6 3.8 fusion.65
  1038.8 7.8 and.445
  1054.9 3.8 fusion.65
  1064.4 22.1 %all_to_all.34 = bf16[4,4,64,12,128]{4,1,3,0,2:T(4,128)(2,1)S(1)} all-to-all(bf16[4,4,64,12,128]{4,1,3,0,2:T(4,128)(2,1)S(1)} %copy.38), channel_id=1, replica_groups=mesh['ta'=4,'ha'=4,'hd'=2] {'hd'}, dimensions={2} | all-to-all | bytes 6291456 | tf_op jit(solution)/shard_map/all_to_all | solution.py:117
  1088.5 4.6 copy.40
  1093.1 6.8 reshape.452
  (687 shorter events, 427.1 us)
Async XLA Ops:
  145.9 6.6 copy-start.6
  156.3 41.5 %copy-start.2 = (bf16[4,4,64,1,12,128]{5,2,4,3,1,0:T(8,128)(2,1)}, bf16[4,4,64,1,12,128]{5,2,4,3,1,0:T(8,128)(2,1)S(1)}, u32[]{:S(2)}) copy-start(bf16[4,4,64,1,12,128]{5,2,4,3,1,0:T(8,128)(2,1)S(1)} %fusion.27) | copy-start | bytes 9437188
  157.2 39.8 %collective-permute-start.1 = (bf16[2,4,64,2,12,128]{5,2,4,3,1,0:T(8,128)(2,1)S(1)}, bf16[2,4,64,2,12,128]{5,2,4,3,1,0:T(8,128)(2,1)S(1)}, u32[]{:S(2)}, u32[]{:S(2)}) collective-permute-start(bf16[2,4,64,2,12,128]{5,2,4,3,1,0:T(8,128)(2,1)S(1)} %get-tuple-element.344), channel_id=1, source_target_pairs={{8,0},{16,8},{24,16},{9,1},{17,9},{25,17},{10,2},{18,10},{26,18},{... | collective-permute-start | bytes 9437192 | tf_op jit(solution)/shard_map/ppermute | solution.py:21
  160.4 37.4 %collective-permute-start = (bf16[2,4,64,2,12,128]{5,2,4,3,1,0:T(8,128)(2,1)S(1)}, bf16[2,4,64,2,12,128]{5,2,4,3,1,0:T(8,128)(2,1)S(1)}, u32[]{:S(2)}, u32[]{:S(2)}) collective-permute-start(bf16[2,4,64,2,12,128]{5,2,4,3,1,0:T(8,128)(2,1)S(1)} %get-tuple-element.343), channel_id=1, source_target_pairs={{0,8},{8,16},{16,24},{1,9},{9,17},{17,25},{2,10},{10,18},{18,26},{... | collective-permute-start | bytes 9437192 | tf_op jit(solution)/shard_map/ppermute | solution.py:20
  197.0 2.5 copy-start.3
  197.8 1.8 copy-start.4
  199.6 14.0 %copy-start.8 = (s32[8]{0:T(128)S(1)}, s32[8]{0:T(128)}, u32[]{:S(2)}) copy-start(s32[8]{0:T(128)} %param.13) | copy-start | bytes 100
  199.6 18.0 %copy-start.7 = (f32[128]{0:T(128)S(1)}, f32[128]{0:T(128)}, u32[]{:S(2)}) copy-start(f32[128]{0:T(128)} %param.9) | copy-start | bytes 1540
  205.5 110.1 %collective-permute-start.3 = (bf16[8,2,64,2,12,128]{5,2,4,3,1,0:T(8,128)(2,1)}, bf16[8,2,64,2,12,128]{5,2,4,3,1,0:T(8,128)(2,1)}, u32[]{:S(2)}, u32[]{:S(2)}) collective-permute-start(bf16[8,2,64,2,12,128]{5,2,4,3,1,0:T(8,128)(2,1)} %get-tuple-element.342), channel_id=1, source_target_pairs={{2,0},{4,2},{6,4},{3,1},{5,3},{7,5},{10,8},{12,10},{14,12},{11,9},... | collective-permute-start | bytes 18874376 | tf_op jit(solution)/shard_map/ppermute | solution.py:21
  206.8 110.6 %collective-permute-start.2 = (bf16[8,2,64,2,12,128]{5,2,4,3,1,0:T(8,128)(2,1)}, bf16[8,2,64,2,12,128]{5,2,4,3,1,0:T(8,128)(2,1)}, u32[]{:S(2)}, u32[]{:S(2)}) collective-permute-start(bf16[8,2,64,2,12,128]{5,2,4,3,1,0:T(8,128)(2,1)} %get-tuple-element.341), channel_id=1, source_target_pairs={{0,2},{2,4},{4,6},{1,3},{3,5},{5,7},{8,10},{10,12},{12,14},{9,11},... | collective-permute-start | bytes 18874376 | tf_op jit(solution)/shard_map/ppermute | solution.py:20
  222.7 111.1 %copy-start.5 = (s32[12,3]{0,1:T(4,128)S(1)}, s32[12,3]{0,1:T(4,128)}, u32[]{:S(2)}) copy-start(s32[12,3]{0,1:T(4,128)} %param.11) | copy-start | bytes 436
  222.7 111.1 %copy-start.9 = (s32[8]{0:T(128)S(1)}, s32[8]{0:T(128)}, u32[]{:S(2)}) copy-start(s32[8]{0:T(128)} %param.12) | copy-start | bytes 100
  352.2 7.4 copy-start.1
  355.4 2.7 copy-start
  382.4 7.4 copy-start.1
  385.6 2.7 copy-start
  412.6 7.4 copy-start.1
  415.8 2.7 copy-start
  442.9 7.4 copy-start.1
  446.1 2.7 copy-start
  473.1 7.4 copy-start.1
  476.3 2.7 copy-start
  503.3 7.4 copy-start.1
  506.5 2.7 copy-start
  533.6 7.4 copy-start.1
  536.8 2.7 copy-start
  563.8 7.4 copy-start.1
  567.0 2.7 copy-start
  594.0 7.4 copy-start.1
  597.2 2.7 copy-start
  624.3 7.4 copy-start.1
  627.5 2.7 copy-start
  654.5 7.4 copy-start.1
  657.7 2.7 copy-start
  684.7 7.4 copy-start.1
  687.9 2.7 copy-start
  715.0 7.4 copy-start.1
  718.2 2.7 copy-start
  745.2 7.4 copy-start.1
  748.4 2.7 copy-start
  775.4 7.4 copy-start.1
  778.6 2.7 copy-start
  805.6 7.4 copy-start.1
  808.8 2.7 copy-start
  835.9 7.4 copy-start.1
  839.1 2.7 copy-start
  866.1 7.4 copy-start.1
  869.3 2.7 copy-start
  896.3 7.4 copy-start.1
  899.5 2.7 copy-start
  926.6 7.4 copy-start.1
  929.8 2.7 copy-start
  956.8 7.4 copy-start.1
  960.0 2.7 copy-start
  987.0 7.4 copy-start.1
  990.2 2.7 copy-start
  1017.3 7.4 copy-start.1
  1020.5 2.7 copy-start
  1047.5 7.4 copy-start.1
  1050.7 2.7 copy-start
where the time goes:
time: 1110 us; the launch traced here: 1100 us
  local copies, waits for them, and re-layouts  442 us (40%)
  matrix products  168 us (15%)
  other arithmetic  162 us (15%)
  blocking collectives  138 us (12%)
  waiting for transfers between devices  129 us (12%)
  loops' own time  46.7 us (4%)
  starting transfers between devices  14.3 us (1%)
    and x24, local copies, waits for them, and re-layouts, attend(): time_mask[:, None, None, :, None, None]  187 us
    ppermute x2, waiting for transfers between devices, extended(): after = lax.ppermute(initial, axis, down)  126 us
    all_to_all x1, blocking collectives, shards(): lax.all_to_all(sectioned, 'hd', split_axis=4, concat_axis=2, tiled=True)  116 us
    dot_general x24, matrix products, attend(): blended = jnp.dot(weights, value_block, preferred_element_type=jnp.float32)  92 us
    dot_general x24, matrix products, attend(): jnp.einsum('qd,kd->qk', query_block, key_block, preferred_element_type=jn...  76.5 us
    while x96, local copies, waits for them, and re-layouts  65.2 us
    slice x24, local copies, waits for them, and re-layouts, attend(): key_block = pair_block[:, :, :, 0, 0].reshape(-1, head_dim)  63.1 us
    another operation x1, loops' own time, shards(): lax.map(attend, jnp.arange(time_tiles * heads_local, dtype=jnp.int32))  46.7 us
  transfers between devices with their start and end apart: 4, of which 4 were waited for; matrix products, arithmetic and copies ran while one was open for 1% of the time, Pallas kernels for 0%

commit v1 on v0

--- a/solution.py
+++ b/solution.py
@@ -1,8 +1,12 @@
+import functools
 import math
 
 import jax
 import jax.numpy as jnp
+import numpy as np
 from jax import lax
+from jax.experimental import pallas as pl
+from jax.experimental.pallas import tpu as pltpu
 from jax.sharding import PartitionSpec as P
 
 TT = 2
@@ -41,7 +45,7 @@
     return grown
 
 
-def shards(qkv, q_gain, k_gain, windows, frame_counts, row_counts):
+def head_shards(qkv, q_gain, k_gain, windows, frame_counts, row_counts):
     frame_num, row_num, col_local, channels = qkv.shape
     head_dim = q_gain.shape[0]
     heads_all = channels // (3 * head_dim)
@@ -118,7 +122,171 @@
     return gathered.reshape(frame_num, row_num, col_local, heads_all * head_dim)
 
 
+MASKED = -1e30
+FEATURES = 128
+
+
+def unit_rms(raw, gain):
+    wide = raw.astype(jnp.float32)
+    meansq = jnp.mean(wide * wide, axis=-1, keepdims=True)
+    return (wide * lax.rsqrt(meansq + 1e-06) * gain).astype(jnp.bfloat16)
+
+
+def attend_kernel(
+    win, flive, rlive, q_ref, ke_ref, ve_ref, ky_ref, vy_ref, kfe_ref, kfy_ref, qf_ref,
+    qg_ref, kg_ref, o_ref, qn, kn, kyn,
+):
+    frames, rows, cols, dim = q_ref.shape
+    halo = ky_ref.shape[1] // (rows + 2 * TH)
+    head = pl.program_id(0)
+    w0, w1, w2 = win[head, 0], win[head, 1], win[head, 2]
+    qg, kg = qg_ref[...], kg_ref[...]
+    for f in range(frames):
+        qn[f] = unit_rms(q_ref[f], qg)
+    for f in range(frames + 2 * TT):
+        kn[f] = unit_rms(ke_ref[f], kg)
+        kyn[f] = unit_rms(ky_ref[f], kg)
+    factor = math.log2(math.e) / math.sqrt(dim)
+
+    def tile(t, r, near_t, near_r):
+        fs = slice(t * TT + TT * (1 - near_t), t * TT + TT * (2 + near_t))
+        r0, r1 = r * TH + TH * (1 - near_r), r * TH + TH * (2 + near_r)
+        rs, ys = slice(r0, r1), slice(r0 * halo, r1 * halo)
+        q = qn[t * TT : (t + 1) * TT, r * TH : (r + 1) * TH].reshape(-1, dim)
+        q = jnp.concatenate([q, qf_ref[w2]], axis=1)
+        nt = (((1,), (1,)), ((), ()))
+        k1 = jnp.concatenate([kn[fs, rs].reshape(-1, dim), kfe_ref[fs, rs].reshape(-1, FEATURES)], axis=1)
+        k2 = jnp.concatenate([kyn[fs, ys].reshape(-1, dim), kfy_ref[fs, ys].reshape(-1, FEATURES)], axis=1)
+        s1 = lax.dot_general(q, k1, nt, preferred_element_type=jnp.float32)
+        s2 = lax.dot_general(q, k2, nt, preferred_element_type=jnp.float32)
+        top = jnp.maximum(jnp.max(s1, axis=1, keepdims=True), jnp.max(s2, axis=1, keepdims=True))
+        p1 = jnp.exp2((s1 - top) * factor)
+        p2 = jnp.exp2((s2 - top) * factor)
+        summed = jnp.sum(p1, axis=1, keepdims=True) + jnp.sum(p2, axis=1, keepdims=True)
+        v1 = ve_ref[fs, rs].reshape(-1, dim)
+        v2 = vy_ref[fs, ys].reshape(-1, dim)
+        out = jnp.dot(p1.astype(jnp.bfloat16), v1, preferred_element_type=jnp.float32)
+        out = out + jnp.dot(p2.astype(jnp.bfloat16), v2, preferred_element_type=jnp.float32)
+        out = (out / summed).reshape(TT, TH, cols, dim)
+        for i in range(TT):
+            for j in range(TH):
+                f, row = t * TT + i, r * TH + j
+                live = (flive[f] * rlive[row]) > 0
+                o_ref[f, row] = jnp.where(live, out[i, j], 0.0).astype(o_ref.dtype)
+
+    for near_t in range(2):
+        for near_r in range(2):
+
+            @pl.when((w0 == near_t) & (w1 == near_r))
+            def _():
+                for t in range(frames // TT):
+                    for r in range(rows // TH):
+                        tile(t, r, near_t, near_r)
+
+
+def attend_call(qkv, ext, side, win, flive, rlive, kfe, kfy, qf, q_gain, k_gain):
+    frames, rows, cols, channels = qkv.shape
+    dim = q_gain.shape[0]
+    heads = channels // (3 * dim)
+    whole = lambda a: pl.BlockSpec(a.shape, lambda h, *_: (0,) * a.ndim)
+    qg, kg = q_gain.reshape(1, dim), k_gain.reshape(1, dim)
+    eb, yb = ext.shape[:3] + (dim,), side.shape[:2] + (dim,)
+    grid_spec = pltpu.PrefetchScalarGridSpec(
+        num_scalar_prefetch=3,
+        grid=(heads,),
+        in_specs=[
+            pl.BlockSpec((frames, rows, cols, dim), lambda h, *_: (0, 0, 0, h)),
+            pl.BlockSpec(eb, lambda h, *_: (0, 0, 0, h)),
+            pl.BlockSpec(eb, lambda h, *_: (0, 0, 0, h + heads)),
+            pl.BlockSpec(yb, lambda h, *_: (0, 0, h)),
+            pl.BlockSpec(yb, lambda h, *_: (0, 0, h + heads)),
+            whole(kfe),
+            whole(kfy),
+            whole(qf),
+            whole(qg),
+            whole(kg),
+        ],
+        out_specs=pl.BlockSpec((frames, rows, cols, dim), lambda h, *_: (0, 0, 0, h)),
+        scratch_shapes=[
+            pltpu.VMEM((frames, rows, cols, dim), jnp.bfloat16),
+            pltpu.VMEM(eb, jnp.bfloat16),
+            pltpu.VMEM(yb, jnp.bfloat16),
+        ],
+    )
+    return pl.pallas_call(
+        attend_kernel,
+        grid_spec=grid_spec,
+        out_shape=jax.ShapeDtypeStruct((frames, rows, cols, heads * dim), jnp.bfloat16),
+        compiler_params=pltpu.CompilerParams(vmem_limit_bytes=40 * 1024 * 1024),
+        cost_estimate=pl.CostEstimate(
+            flops=4 * heads * frames * rows * cols * 1440 * dim,
+            bytes_accessed=ext.size * 2 + side.size * 2 + qkv.size,
+            transcendentals=heads * frames * rows * cols * 1440,
+        ),
+    )(win, flive, rlive, qkv, ext, ext, side, side, kfe, kfy, qf, qg, kg)
+
+
+def shift(value, axis, step):
+    size = lax.axis_size(axis)
+    pairs = [(i, i + step) for i in range(size) if 0 <= i + step < size]
+    return lax.ppermute(value, axis, pairs)
+
+
+def tables(frames, rows, cols, windows, frame_counts, row_counts):
+    swap = [(0, 1), (1, 0)]
+    me = lax.axis_index("hd")
+    other = lax.ppermute(windows, "hd", swap)
+    win = jnp.where(me == 0, jnp.concatenate([windows, other]), jnp.concatenate([other, windows]))
+    at_f = lax.axis_index("ta") * frames - TT + jnp.arange(frames + 2 * TT, dtype=jnp.int32)
+    at_r = lax.axis_index("ha") * rows - TH + jnp.arange(rows + 2 * TH, dtype=jnp.int32)
+    flive = valid_cells(at_f, TT, frame_counts)
+    rlive = valid_cells(at_r, TH, row_counts)
+    live = flive[:, None] & rlive[None, :]
+    own = (me * cols + jnp.arange(cols, dtype=jnp.int32)) // TW
+    beside = jnp.full((TW,), jnp.where(me == 0, cols // TW, cols // TW - 1), jnp.int32)
+    lanes = jnp.arange(FEATURES, dtype=jnp.int32)
+
+    def key_entries(tiles):
+        hot = (tiles[:, None] == lanes[None, :])[None, None]
+        dead = (~live)[:, :, None, None] & (lanes == FEATURES - 1)
+        return jnp.where(hot | dead, 1.0, 0.0).astype(jnp.bfloat16)
+
+    kfe = key_entries(own)
+    kfy = key_entries(beside).reshape(frames + 2 * TT, (rows + 2 * TH) * TW, FEATURES)
+    gap = jnp.abs(own[:, None] - lanes[None, :])
+    far = jnp.stack([gap > 0, gap > 1]) | (lanes == FEATURES - 1)
+    qf = jnp.where(far, MASKED, 0.0).astype(jnp.bfloat16)
+    qf = jnp.broadcast_to(qf[:, None], (2, TT * TH, cols, FEATURES)).reshape(2, -1, FEATURES)
+    count = lambda flags, width: flags.astype(jnp.int32)[width:-width]
+    return win, count(flive, TT), count(rlive, TH), kfe, kfy, qf
+
+
+def column_shards(qkv, q_gain, k_gain, windows, frame_counts, row_counts):
+    frames, rows, cols, channels = qkv.shape
+    kv = qkv[..., channels // 3 :]
+    me = lax.axis_index("hd")
+    edge = lax.dynamic_slice_in_dim(kv, jnp.where(me == 0, cols - TW, 0), TW, axis=2)
+    side = lax.ppermute(edge, "hd", [(0, 1), (1, 0)])
+
+    def grown(value):
+        lo = shift(value[:, rows - TH :], "ha", 1)
+        hi = shift(value[:, :TH], "ha", -1)
+        value = jnp.concatenate([lo, value, hi], axis=1)
+        lo = shift(value[frames - TT :], "ta", 1)
+        hi = shift(value[:TT], "ta", -1)
+        return jnp.concatenate([lo, value, hi], axis=0)
+
+    ext = grown(kv)
+    side = grown(side).reshape(frames + 2 * TT, -1, kv.shape[-1])
+    made = tables(frames, rows, cols, windows, frame_counts, row_counts)
+    return attend_call(qkv, ext, side, *made, q_gain, k_gain)
+
+
 def solution(mesh):
+    def shards(qkv, *rest):
+        fits = mesh.shape["hd"] == 2 and qkv.shape[2] % 16 == 0
+        return (column_shards if fits else head_shards)(qkv, *rest)
+
     return jax.shard_map(
         shards,
         mesh=mesh,

time: 1110 us -> 268 us (0.24)
  local copies, waits for them, and re-layouts: 442 us -> 26.4 us
  matrix products: 168 us -> 0 us
  blocking collectives: 138 us -> 0 us
  other arithmetic: 162 us -> 30 us
  Pallas kernels: 0 us -> 57.6 us
  loops' own time: 46.7 us -> 0 us
  starting transfers between devices: 14.3 us -> 28 us
    and x48 -> x0, local copies, waits for them, and re-layouts: 189 us -> none  [the longest x24 187 us: attend(): time_mask[:, None, None, :, None, None]]
    dot_general x48 -> x0, matrix products: 168 us -> none  [the longest x24 92 us: attend(): blended = jnp.dot(weights, value_block, preferred_element_type=jnp.float32)]
    all_to_all x2 -> x0, blocking collectives: 138 us -> none  [the longest x1 116 us: shards(): lax.all_to_all(sectioned, 'hd', split_axis=4, concat_axis=2, tiled=True)]
    and x144 -> x1, other arithmetic: 77.1 us -> 0.08 us  [key_entries(): dead = (~live)[:, :, None, None] & (lanes == FEATURES - 1)]
    slice x50 -> x5, local copies, waits for them, and re-layouts: 85.2 us -> 19.1 us  [the longest x2 7.64 us: grown(): lo = shift(value[frames - TT:], 'ta', 1)]
    while x96 -> x0, local copies, waits for them, and re-layouts: 65.2 us -> none
    pallas_call x0 -> x1, Pallas kernels: none -> 57.6 us  [attend_call(): pl.pallas_call(attend_kernel, grid_spec=grid_spec, out_shape=jax.ShapeDty...]
    another operation x1 -> x0, loops' own time: 46.7 us -> none  [shards(): lax.map(attend, jnp.arange(time_tiles * heads_local, dtype=jnp.int32))]
  transfers between devices with their start and end apart: 4 -> 10, of which waited for: 4 -> 6; matrix products, arithmetic and copies ran while one was open for 1% -> 11% of each run, Pallas kernels for 0% -> 0%
where the time goes in v1:
time: 268 us; the launch traced here: 267 us
  waiting for transfers between devices  125 us (47%)
  Pallas kernels  57.6 us (21%)
  other arithmetic  30 us (11%)
  starting transfers between devices  28 us (10%)
  local copies, waits for them, and re-layouts  26.4 us (10%)
    ppermute x8, waiting for transfers between devices, shift(): return lax.ppermute(value, axis, pairs)  92.1 us
    pallas_call x1, Pallas kernels, attend_call(): pl.pallas_call(attend_kernel, grid_spec=grid_spec, out_shape=jax.ShapeDty...  57.6 us
    ppermute x1, waiting for transfers between devices, column_shards(): side = lax.ppermute(edge, 'hd', [(0, 1), (1, 0)])  33.1 us
    ppermute x8, starting transfers between devices, shift(): return lax.ppermute(value, axis, pairs)  26.5 us
    concatenate x1, other arithmetic, grown(): return jnp.concatenate([lo, value, hi], axis=0)  17.4 us
    slice x2, local copies, waits for them, and re-layouts, grown(): lo = shift(value[frames - TT:], 'ta', 1)  7.64 us
    slice x1, local copies, waits for them, and re-layouts, grown(): lo = shift(value[:, rows - TH:], 'ha', 1)  6.79 us
    reshape x1, other arithmetic, column_shards(): side = grown(side).reshape(frames + 2 * TT, -1, kv.shape[-1])  5.81 us
  transfers between devices with their start and end apart: 10, of which 6 were waited for; matrix products, arithmetic and copies ran while one was open for 11% of the time, Pallas kernels for 0%

profile of v1, /device:TPU:1, one launch (start us, length us, event | category | flops | bytes accessed | tf_op | source)
XLA Modules:
  0.0 267.5 jit_solution(11687996141546164965)
XLA Ops:
  0.0 0.0 copy-start.3
  0.0 6.8 %fusion.5 = (bf16[4,2,32,6144]{3,2,1,0:T(8,128)(2,1)}, bf16[4,2,32,6144]{3,2,1,0:T(8,128)(2,1)}) fusion(bf16[4,4,32,9216]{3,2,1,0:T(8,128)(2,1)} %q_ref.1), kind=kLoop, calls=%fused_computation.48 | loop fusion | bytes 12582912 | tf_op jit(solution)/shard_map/slice | solution.py:272
  6.8 1.3 collective-permute-start.2
  8.1 6.3 %collective-permute-start.1 = (bf16[4,2,32,6144]{3,2,1,0:T(8,128)(2,1)}, bf16[4,2,32,6144]{3,2,1,0:T(8,128)(2,1)}, u32[]{:S(2)}, u32[]{:S(2)}) collective-permute-start(bf16[4,2,32,6144]{3,2,1,0:T(8,128)(2,1)} %get-tuple-element.7), channel_id=1, source_target_pairs={{0,2},{2,4},{4,6},{1,3},{3,5},{5,7},{8,10},{10,12},{12,14},{9,11},... | collective-permute-start | bytes 9437192 | tf_op jit(solution)/shard_map/ppermute | solution.py:232
  14.4 0.0 copy-done.3
  14.4 0.0 copy-start.6
  14.4 0.0 copy-start.7
  14.4 0.0 copy-start.8
  14.4 3.1 %slice.44 = bf16[4,4,32,6144]{3,2,1,0:T(8,128)(2,1)} slice(bf16[4,4,32,9216]{3,2,1,0:T(8,128)(2,1)S(1)} %copy-done.3), slice={[0:4], [0:4], [0:32], [3072:9216]} | slice | bytes 12582912 | tf_op jit(solution)/shard_map/slice | solution.py:266
  17.5 2.7 %constant_dynamic-slice_fusion = bf16[4,4,8,6144]{3,2,1,0:T(8,128)(2,1)} fusion(bf16[4,4,32,6144]{3,2,1,0:T(8,128)(2,1)} %slice.44, s32[]{:T(128)S(6)} %select_n.92), kind=kLoop, calls=%fused_computation.46 | loop fusion | bytes 3145732 | tf_op jit(solution)/shard_map/dynamic_slice | solution.py:268
  20.2 1.4 collective-permute-start.5
  21.6 0.0 copy-done.6
  21.6 0.1 collective-permute-start
  21.8 0.0 copy-done.7
  21.8 0.2 select_reduce_fusion.1
  21.9 0.0 copy-done.8
  22.0 0.2 select_reduce_fusion
  22.2 0.1 slice_convert_fusion.1.flive
  22.2 0.1 and_not_fusion
  22.3 0.1 iota_compare_fusion
  22.4 33.1 %collective-permute-done.5 = bf16[4,4,8,6144]{3,2,1,0:T(8,128)(2,1)} collective-permute-done((bf16[4,4,8,6144]{3,2,1,0:T(8,128)(2,1)}, bf16[4,4,8,6144]{3,2,1,0:T(8,128)(2,1)}, u32[]{:S(2)}, u32[]{:S(2)}) %collective-permute-start.5) | collective-permute-done | bytes 1572896 | tf_op jit(solution)/shard_map/ppermute | solution.py:269
  55.5 1.5 fusion.7
  57.0 1.5 collective-permute-start.6
  58.5 20.3 %collective-permute-done.2 = bf16[4,2,32,6144]{3,2,1,0:T(8,128)(2,1)S(1)} collective-permute-done((bf16[4,2,32,6144]{3,2,1,0:T(8,128)(2,1)}, bf16[4,2,32,6144]{3,2,1,0:T(8,128)(2,1)S(1)}, u32[]{:S(2)}, u32[]{:S(2)}) %collective-permute-start.2) | collective-permute-done | bytes 3145760 | tf_op jit(solution)/shard_map/ppermute | solution.py:232
  78.8 0.0 copy-start.5
  78.8 1.0 collective-permute-done.1
  79.8 5.6 %pad_maximum_fusion.1 = bf16[4,8,32,6144]{3,2,1,0:T(8,128)(2,1)S(1)} fusion(bf16[4,2,32,6144]{3,2,1,0:T(8,128)(2,1)S(1)} %collective-permute-done.2, bf16[4,4,32,6144]{3,2,1,0:T(8,128)(2,1)} %slice.44, bf16[4,2,32,6144]{3,2,1,0:T(8,128)(2,1)} %collective-permute-done.1), kind=kLoop, calls=%fused_computation.1 | loop fusion | flops 12582912 | bytes 25165824 | tf_op jit(solution)/shard_map/concatenate | solution.py:274
  85.4 0.0 copy-done.5
  85.5 5.3 %fusion.4 = (bf16[2,8,32,6144]{3,2,1,0:T(8,128)(2,1)}, bf16[2,8,32,6144]{3,2,1,0:T(8,128)(2,1)}) fusion(bf16[4,8,32,6144]{3,2,1,0:T(8,128)(2,1)S(1)} %pad_maximum_fusion.1), kind=kLoop, calls=%fused_computation.47 | loop fusion | bytes 25165824 | tf_op jit(solution)/shard_map/slice | solution.py:275
  90.8 4.5 %collective-permute-start.4 = (bf16[2,8,32,6144]{3,2,1,0:T(8,128)(2,1)}, bf16[2,8,32,6144]{3,2,1,0:T(8,128)(2,1)}, u32[]{:S(2)}, u32[]{:S(2)}) collective-permute-start(bf16[2,8,32,6144]{3,2,1,0:T(8,128)(2,1)} %get-tuple-element.6), channel_id=1, source_target_pairs={{8,0},{16,8},{24,16},{9,1},{17,9},{25,17},{10,2},{18,10},{26,18},{... | collective-permute-start | bytes 18874376 | tf_op jit(solution)/shard_map/ppermute | solution.py:232
  95.3 3.5 %collective-permute-start.3 = (bf16[2,8,32,6144]{3,2,1,0:T(8,128)(2,1)}, bf16[2,8,32,6144]{3,2,1,0:T(8,128)(2,1)}, u32[]{:S(2)}, u32[]{:S(2)}) collective-permute-start(bf16[2,8,32,6144]{3,2,1,0:T(8,128)(2,1)} %get-tuple-element.5), channel_id=1, source_target_pairs={{0,8},{8,16},{16,24},{1,9},{9,17},{17,25},{2,10},{10,18},{18,26},{... | collective-permute-start | bytes 18874376 | tf_op jit(solution)/shard_map/ppermute | solution.py:232
  98.8 0.1 fusion.1
  98.9 1.3 collective-permute-start.7
  100.2 0.0 collective-permute-done.6
  100.2 0.1 constant_dynamic-update-slice_fusion.2
  100.2 1.5 constant_dynamic-update-slice_fusion.1
  101.8 17.5 %collective-permute-done.7 = bf16[4,2,8,6144]{3,2,1,0:T(8,128)(2,1)S(1)} collective-permute-done((bf16[4,2,8,6144]{3,2,1,0:T(8,128)(2,1)S(1)}, bf16[4,2,8,6144]{3,2,1,0:T(8,128)(2,1)S(1)}, u32[]{:S(2)}, u32[]{:S(2)}) %collective-permute-start.7) | collective-permute-done | bytes 786464 | tf_op jit(solution)/shard_map/ppermute | solution.py:232
  119.3 0.1 constant_dynamic-update-slice_fusion
  119.3 0.0 copy-start.4
  119.3 2.3 fusion.6
  121.7 4.1 %collective-permute-start.9 = (bf16[2,8,8,6144]{3,2,1,0:T(8,128)(2,1)}, bf16[2,8,8,6144]{3,2,1,0:T(8,128)(2,1)S(1)}, u32[]{:S(2)}, u32[]{:S(2)}) collective-permute-start(bf16[2,8,8,6144]{3,2,1,0:T(8,128)(2,1)} %get-tuple-element.10), channel_id=1, source_target_pairs={{8,0},{16,8},{24,16},{9,1},{17,9},{25,17},{10,2},{18,10},{26,18},{... | collective-permute-start | bytes 4718600 | tf_op jit(solution)/shard_map/ppermute | solution.py:232
  125.8 4.0 %collective-permute-start.8 = (bf16[2,8,8,6144]{3,2,1,0:T(8,128)(2,1)}, bf16[2,8,8,6144]{3,2,1,0:T(8,128)(2,1)}, u32[]{:S(2)}, u32[]{:S(2)}) collective-permute-start(bf16[2,8,8,6144]{3,2,1,0:T(8,128)(2,1)} %get-tuple-element.9), channel_id=1, source_target_pairs={{0,8},{8,16},{16,24},{1,9},{9,17},{17,25},{2,10},{10,18},{18,26},{... | collective-permute-start | bytes 4718600 | tf_op jit(solution)/shard_map/ppermute | solution.py:232
  129.8 0.1 broadcast_and_fusion
  129.9 0.1 select_convert_fusion.1.kfy_ref
  130.0 0.0 copy-done.4
  130.0 0.2 select_convert_fusion.kfe_ref
  130.1 0.1 slice_convert_fusion.rlive
  130.2 0.0 collective-permute-done
  130.2 0.1 pad_add_fusion.1
  130.3 0.1 copy.12
  130.4 0.1 copy.13
  130.5 52.1 %collective-permute-done.9 = bf16[2,8,8,6144]{3,2,1,0:T(8,128)(2,1)S(1)} collective-permute-done((bf16[2,8,8,6144]{3,2,1,0:T(8,128)(2,1)}, bf16[2,8,8,6144]{3,2,1,0:T(8,128)(2,1)S(1)}, u32[]{:S(2)}, u32[]{:S(2)}) %collective-permute-start.9) | collective-permute-done | bytes 1572896 | tf_op jit(solution)/shard_map/ppermute | solution.py:232
  182.6 1.3 collective-permute-done.8
  183.8 5.8 %maximum_bitcast_fusion.ky_ref.vy_ref = bf16[8,64,6144]{2,1,0:T(8,128)(2,1)} fusion(bf16[2,8,8,6144]{3,2,1,0:T(8,128)(2,1)S(1)} %collective-permute-done.9, bf16[4,8,8,6144]{3,2,1,0:T(8,128)(2,1)} %copy-done.4, bf16[2,8,8,6144]{3,2,1,0:T(8,128)(2,1)} %collective-permute-done.8), kind=kLoop, calls=%fused_computation.2 | loop fusion | flops 6291456 | bytes 12582912 | tf_op jit(solution)/shard_map/reshape | solution.py:280
  189.7 0.0 copy-start.1
  189.7 0.0 copy-start.2
  189.7 0.0 collective-permute-done.4
  189.7 0.0 collective-permute-done.3
  189.7 17.4 %pad_maximum_fusion.ke_ref.ve_ref = bf16[8,8,32,6144]{3,2,1,0:T(8,128)(2,1)} fusion(bf16[2,8,32,6144]{3,2,1,0:T(8,128)(2,1)} %collective-permute-done.4, bf16[4,2,32,6144]{3,2,1,0:T(8,128)(2,1)} %copy-done.5, bf16[4,4,32,6144]{3,2,1,0:T(8,128)(2,1)} %slice.44, bf16[4,2,32,6144]{3,2,1,0:T(8,128)(2,1)} %collective-permute-done.1, ...), kind=kLoop, calls=%fused_computation | loop fusion | flops 50331648 | bytes 50331648 | tf_op jit(solution)/shard_map/concatenate | solution.py:277
  207.1 0.0 copy-done.1
  207.1 0.0 copy-done.2
  207.1 0.0 copy-start
  207.1 2.8 %copy-done = bf16[8,64,6144]{2,1,0:T(8,128)(2,1)S(1)} copy-done((bf16[8,64,6144]{2,1,0:T(8,128)(2,1)S(1)}, bf16[8,64,6144]{2,1,0:T(8,128)(2,1)}, u32[]{:S(2)}) %copy-start) | copy-done | bytes 6291480
  209.9 57.6 %shard_map.64 = bf16[4,4,32,3072]{3,2,1,0:T(8,128)(2,1)} custom-call(s32[24,3]{1,0:T(8,128)S(1)} %broadcast_select_fusion.win, s32[4]{0:T(128)S(1)} %slice_convert_fusion.1.flive, s32[4]{0:T(128)S(1)} %slice_convert_fusion.rlive, bf16[4,4,32,9216]{3,2,1,0:T(8,128)(2,1)} %q_ref.1, bf16[8,8,32,6144]{3,2,1,0:T(8,128)(2,1)} %pad_maximum_fusion.ke_ref.ve_ref, ...), custom_call_target="tpu_custom_call" | custom-call | flops 9059696640 | bytes 36175872 | tf_op jit(solution)/shard_map/pallas_call | solution.py:216
  (9 shorter events, 0.1 us)
Async XLA Ops:
  0.0 14.4 %copy-start.3 = (bf16[4,4,32,9216]{3,2,1,0:T(8,128)(2,1)S(1)}, bf16[4,4,32,9216]{3,2,1,0:T(8,128)(2,1)}, u32[]{:S(2)}) copy-start(bf16[4,4,32,9216]{3,2,1,0:T(8,128)(2,1)} %q_ref.1) | copy-start | bytes 28311556
  6.8 72.1 %collective-permute-start.2 = (bf16[4,2,32,6144]{3,2,1,0:T(8,128)(2,1)}, bf16[4,2,32,6144]{3,2,1,0:T(8,128)(2,1)S(1)}, u32[]{:S(2)}, u32[]{:S(2)}) collective-permute-start(bf16[4,2,32,6144]{3,2,1,0:T(8,128)(2,1)} %get-tuple-element.8), channel_id=1, source_target_pairs={{2,0},{4,2},{6,4},{3,1},{5,3},{7,5},{10,8},{12,10},{14,12},{11,9},... | collective-permute-start | bytes 9437192 | tf_op jit(solution)/shard_map/ppermute | solution.py:232
  8.1 71.7 %collective-permute-start.1 = (bf16[4,2,32,6144]{3,2,1,0:T(8,128)(2,1)}, bf16[4,2,32,6144]{3,2,1,0:T(8,128)(2,1)}, u32[]{:S(2)}, u32[]{:S(2)}) collective-permute-start(bf16[4,2,32,6144]{3,2,1,0:T(8,128)(2,1)} %get-tuple-element.7), channel_id=1, source_target_pairs={{0,2},{2,4},{4,6},{1,3},{3,5},{5,7},{8,10},{10,12},{12,14},{9,11},... | collective-permute-start | bytes 9437192 | tf_op jit(solution)/shard_map/ppermute | solution.py:232
  14.4 7.3 %copy-start.6 = (s32[12,3]{0,1:T(4,128)S(1)}, s32[12,3]{0,1:T(4,128)}, u32[]{:S(2)}) copy-start(s32[12,3]{0,1:T(4,128)} %param.9) | copy-start | bytes 436
  14.4 7.4 %copy-start.7 = (s32[8]{0:T(128)S(1)}, s32[8]{0:T(128)}, u32[]{:S(2)}) copy-start(s32[8]{0:T(128)} %param.10) | copy-start | bytes 100
  14.4 7.6 %copy-start.8 = (s32[8]{0:T(128)S(1)}, s32[8]{0:T(128)}, u32[]{:S(2)}) copy-start(s32[8]{0:T(128)} %param.11) | copy-start | bytes 100
  20.2 35.3 %collective-permute-start.5 = (bf16[4,4,8,6144]{3,2,1,0:T(8,128)(2,1)}, bf16[4,4,8,6144]{3,2,1,0:T(8,128)(2,1)}, u32[]{:S(2)}, u32[]{:S(2)}) collective-permute-start(bf16[4,4,8,6144]{3,2,1,0:T(8,128)(2,1)} %constant_dynamic-slice_fusion), channel_id=1, source_target_pairs={{0,1},{1,0},{2,3},{3,2},{4,5},{5,4},{6,7},{7,6},{8,9},{9,8},{10,11... | collective-permute-start | bytes 4718600 | tf_op jit(solution)/shard_map/ppermute | solution.py:269
  21.6 108.6 %collective-permute-start = (s32[12,3]{0,1:T(4,128)S(1)}, s32[12,3]{0,1:T(4,128)S(1)}, u32[]{:S(2)}, u32[]{:S(2)}) collective-permute-start(s32[12,3]{0,1:T(4,128)S(1)} %copy-done.6), channel_id=1, source_target_pairs={{0,1},{1,0},{2,3},{3,2},{4,5},{5,4},{6,7},{7,6},{8,9},{9,8},{10,11... | collective-permute-start | bytes 440 | tf_op jit(solution)/shard_map/ppermute | solution.py:238
  57.0 43.2 %collective-permute-start.6 = (bf16[4,2,8,6144]{3,2,1,0:T(8,128)(2,1)S(1)}, bf16[4,2,8,6144]{3,2,1,0:T(8,128)(2,1)S(1)}, u32[]{:S(2)}, u32[]{:S(2)}) collective-permute-start(bf16[4,2,8,6144]{3,2,1,0:T(8,128)(2,1)S(1)} %get-tuple-element.12), channel_id=1, source_target_pairs={{0,2},{2,4},{4,6},{1,3},{3,5},{5,7},{8,10},{10,12},{12,14},{9,11},... | collective-permute-start | bytes 2359304 | tf_op jit(solution)/shard_map/ppermute | solution.py:232
  78.8 6.6 %copy-start.5 = (bf16[4,2,32,6144]{3,2,1,0:T(8,128)(2,1)}, bf16[4,2,32,6144]{3,2,1,0:T(8,128)(2,1)S(1)}, u32[]{:S(2)}) copy-start(bf16[4,2,32,6144]{3,2,1,0:T(8,128)(2,1)S(1)} %collective-permute-done.2) | copy-start | bytes 9437188
  90.8 98.9 %collective-permute-start.4 = (bf16[2,8,32,6144]{3,2,1,0:T(8,128)(2,1)}, bf16[2,8,32,6144]{3,2,1,0:T(8,128)(2,1)}, u32[]{:S(2)}, u32[]{:S(2)}) collective-permute-start(bf16[2,8,32,6144]{3,2,1,0:T(8,128)(2,1)} %get-tuple-element.6), channel_id=1, source_target_pairs={{8,0},{16,8},{24,16},{9,1},{17,9},{25,17},{10,2},{18,10},{26,18},{... | collective-permute-start | bytes 18874376 | tf_op jit(solution)/shard_map/ppermute | solution.py:232
  95.3 94.4 %collective-permute-start.3 = (bf16[2,8,32,6144]{3,2,1,0:T(8,128)(2,1)}, bf16[2,8,32,6144]{3,2,1,0:T(8,128)(2,1)}, u32[]{:S(2)}, u32[]{:S(2)}) collective-permute-start(bf16[2,8,32,6144]{3,2,1,0:T(8,128)(2,1)} %get-tuple-element.5), channel_id=1, source_target_pairs={{0,8},{8,16},{16,24},{1,9},{9,17},{17,25},{2,10},{10,18},{18,26},{... | collective-permute-start | bytes 18874376 | tf_op jit(solution)/shard_map/ppermute | solution.py:232
  98.9 20.4 %collective-permute-start.7 = (bf16[4,2,8,6144]{3,2,1,0:T(8,128)(2,1)S(1)}, bf16[4,2,8,6144]{3,2,1,0:T(8,128)(2,1)S(1)}, u32[]{:S(2)}, u32[]{:S(2)}) collective-permute-start(bf16[4,2,8,6144]{3,2,1,0:T(8,128)(2,1)S(1)} %get-tuple-element.11), channel_id=1, source_target_pairs={{2,0},{4,2},{6,4},{3,1},{5,3},{7,5},{10,8},{12,10},{14,12},{11,9},... | collective-permute-start | bytes 2359304 | tf_op jit(solution)/shard_map/ppermute | solution.py:232
  119.3 10.6 %copy-start.4 = (bf16[4,8,8,6144]{3,2,1,0:T(8,128)(2,1)}, bf16[4,8,8,6144]{3,2,1,0:T(8,128)(2,1)S(1)}, u32[]{:S(2)}) copy-start(bf16[4,8,8,6144]{3,2,1,0:T(8,128)(2,1)S(1)} %constant_dynamic-update-slice_fusion) | copy-start | bytes 9437188
  121.7 60.9 %collective-permute-start.9 = (bf16[2,8,8,6144]{3,2,1,0:T(8,128)(2,1)}, bf16[2,8,8,6144]{3,2,1,0:T(8,128)(2,1)S(1)}, u32[]{:S(2)}, u32[]{:S(2)}) collective-permute-start(bf16[2,8,8,6144]{3,2,1,0:T(8,128)(2,1)} %get-tuple-element.10), channel_id=1, source_target_pairs={{8,0},{16,8},{24,16},{9,1},{17,9},{25,17},{10,2},{18,10},{26,18},{... | collective-permute-start | bytes 4718600 | tf_op jit(solution)/shard_map/ppermute | solution.py:232
  125.8 58.1 %collective-permute-start.8 = (bf16[2,8,8,6144]{3,2,1,0:T(8,128)(2,1)}, bf16[2,8,8,6144]{3,2,1,0:T(8,128)(2,1)}, u32[]{:S(2)}, u32[]{:S(2)}) collective-permute-start(bf16[2,8,8,6144]{3,2,1,0:T(8,128)(2,1)} %get-tuple-element.9), channel_id=1, source_target_pairs={{0,8},{8,16},{16,24},{1,9},{9,17},{17,25},{2,10},{10,18},{18,26},{... | collective-permute-start | bytes 4718600 | tf_op jit(solution)/shard_map/ppermute | solution.py:232
  189.7 17.4 %copy-start.1 = (f32[128]{0:T(128)S(1)}, f32[128]{0:T(128)}, u32[]{:S(2)}) copy-start(f32[128]{0:T(128)} %param.7) | copy-start | bytes 1540
  189.7 17.4 %copy-start.2 = (f32[128]{0:T(128)S(1)}, f32[128]{0:T(128)}, u32[]{:S(2)}) copy-start(f32[128]{0:T(128)} %param.8) | copy-start | bytes 1540
  207.1 2.8 %copy-start = (bf16[8,64,6144]{2,1,0:T(8,128)(2,1)S(1)}, bf16[8,64,6144]{2,1,0:T(8,128)(2,1)}, u32[]{:S(2)}) copy-start(bf16[8,64,6144]{2,1,0:T(8,128)(2,1)} %maximum_bitcast_fusion.ky_ref.vy_ref) | copy-start | bytes 18874372

commit v2 on v1

--- a/solution.py
+++ b/solution.py
@@ -261,31 +261,182 @@
     return win, count(flive, TT), count(rlive, TH), kfe, kfy, qf
 
 
-def column_shards(qkv, q_gain, k_gain, windows, frame_counts, row_counts):
+CHUNKS = 6
+MESH = pl.DeviceIdType.MESH
+Y_OWN, Z_UP, Z_DOWN, ZS_UP, ZS_DOWN, X_UP, X_DOWN, XLO_UP, XLO_DOWN, XHI_UP, XHI_DOWN, XS_UP, XS_DOWN = range(13)
+KINDS = 13
+
+
+def halo_kernel(sizes, base, qkv, edge, ext, side, send_sem, recv_sem, own_sem):
+    frames, rows = qkv.shape[:2]
+    f1, r1 = frames + TT, rows + TH
+    width = ext.shape[-1] // CHUNKS
+    at = {axis: lax.axis_index(axis) for axis in sizes}
+    up = {axis: at[axis] < sizes[axis] - 1 for axis in ("ta", "ha")}
+    down = {axis: at[axis] > 0 for axis in ("ta", "ha")}
+    partner = {"hd": 1 - at["hd"]}
+
+    barrier = pltpu.get_barrier_semaphore()
+    pl.semaphore_signal(barrier, inc=1, device_id=partner, device_id_type=MESH)
+    for axis in ("ta", "ha"):
+        for there, step in ((up[axis], 1), (down[axis], -1)):
+
+            @pl.when(there)
+            def _():
+                pl.semaphore_signal(barrier, inc=1, device_id={axis: at[axis] + step}, device_id_type=MESH)
+
+    greeted = 1
+    for axis in ("ta", "ha"):
+        greeted = greeted + up[axis].astype(jnp.int32) + down[axis].astype(jnp.int32)
+    pl.semaphore_wait(barrier, greeted)
+
+    def lanes(c):
+        return pl.ds(c * width, width)
+
+    def own(fs, rs, c):
+        return qkv.at[fs, rs, :, pl.ds(base + c * width, width)]
+
+    def cells(fs, rs, c):
+        return ext.at[fs, rs, :, lanes(c)]
+
+    def strip(fs, rs, c, ref=side):
+        return ref.at[fs, slice(rs.start * TW, rs.stop * TW), lanes(c)]
+
+    def remote(kind, c, src, dst, device):
+        return pltpu.make_async_remote_copy(
+            src_ref=src, dst_ref=dst, send_sem=send_sem.at[kind, c], recv_sem=recv_sem.at[kind, c],
+            device_id=device, device_id_type=MESH,
+        )
+
+    F, R = slice(TT, f1), slice(TH, r1)
+    LO, HI = slice(0, TT), slice(f1, f1 + TT)
+    RLO, RHI = slice(0, TH), slice(r1, r1 + TH)
+    OF = slice(0, frames)
+    first, last = slice(0, TT), slice(frames - TT, frames)
+    rfirst, rlast = slice(0, TH), slice(rows - TH, rows)
+    flast, ffirst = slice(frames, f1), slice(TT, 2 * TT)
+    ROWS_ALL = slice(0, rows + 2 * TH)
+
+    def plan(kind, c):
+        return {
+            Z_UP: ("ha", 1, own(OF, rlast, c), cells(F, RLO, c), own(OF, rfirst, c)),
+            Z_DOWN: ("ha", -1, own(OF, rfirst, c), cells(F, RHI, c), own(OF, rfirst, c)),
+            ZS_UP: ("ha", 1, strip(F, slice(rows, r1), c), strip(F, RLO, c), strip(OF, rfirst, c, edge)),
+            ZS_DOWN: ("ha", -1, strip(F, slice(TH, 2 * TH), c), strip(F, RHI, c), strip(OF, rfirst, c, edge)),
+            X_UP: ("ta", 1, own(last, slice(0, rows), c), cells(LO, R, c), own(first, slice(0, rows), c)),
+            X_DOWN: ("ta", -1, own(first, slice(0, rows), c), cells(HI, R, c), own(first, slice(0, rows), c)),
+            XLO_UP: ("ta", 1, cells(flast, RLO, c), cells(LO, RLO, c), own(first, rfirst, c)),
+            XLO_DOWN: ("ta", -1, cells(ffirst, RLO, c), cells(HI, RLO, c), own(first, rfirst, c)),
+            XHI_UP: ("ta", 1, cells(flast, RHI, c), cells(LO, RHI, c), own(first, rfirst, c)),
+            XHI_DOWN: ("ta", -1, cells(ffirst, RHI, c), cells(HI, RHI, c), own(first, rfirst, c)),
+            XS_UP: ("ta", 1, strip(flast, ROWS_ALL, c), strip(LO, ROWS_ALL, c), None),
+            XS_DOWN: ("ta", -1, strip(ffirst, ROWS_ALL, c), strip(HI, ROWS_ALL, c), None),
+        }[kind]
+
+    def start(kind, c):
+        axis, step, src, dst, fill = plan(kind, c)
+        if fill is None:
+            fill = strip(ffirst, ROWS_ALL, c)
+        sends, gets = (up, down) if step == 1 else (down, up)
+
+        @pl.when(sends[axis])
+        def _():
+            remote(kind, c, src, dst, {axis: at[axis] + step}).start()
+
+        @pl.when(jnp.logical_not(gets[axis]))
+        def _():
+            pltpu.make_async_copy(fill, dst, recv_sem.at[kind, c]).start()
+
+    def got(kind, c):
+        dst = plan(kind, c)[3]
+        pltpu.make_async_copy(dst, dst, recv_sem.at[kind, c]).wait()
+
+    def sent(kind, c):
+        axis, step, src, dst, _ = plan(kind, c)
+
+        @pl.when((up if step == 1 else down)[axis])
+        def _():
+            remote(kind, c, src, dst, {axis: at[axis] + step}).wait_send()
+
+    def y_copy(c):
+        return remote(Y_OWN, c, strip(OF, slice(0, rows), c, edge), strip(F, R, c), partner)
+
+    def home(c):
+        return pltpu.make_async_copy(own(OF, slice(0, rows), c), cells(F, R, c), own_sem.at[c])
+
+    ahead = 2
+    for c in range(CHUNKS):
+        y_copy(c).start()
+    for c in range(CHUNKS + ahead):
+        if c < CHUNKS:
+            for kind in (Z_UP, Z_DOWN, X_UP, X_DOWN):
+                start(kind, c)
+            home(c).start()
+        d = c - 1
+        if 0 <= d < CHUNKS:
+            y_copy(d).wait_recv()
+            start(ZS_UP, d)
+            start(ZS_DOWN, d)
+        e = c - ahead
+        if 0 <= e < CHUNKS:
+            got(Z_UP, e)
+            start(XLO_UP, e)
+            start(XLO_DOWN, e)
+            got(Z_DOWN, e)
+            start(XHI_UP, e)
+            start(XHI_DOWN, e)
+            got(ZS_UP, e)
+            got(ZS_DOWN, e)
+            start(XS_UP, e)
+            start(XS_DOWN, e)
+    for c in range(CHUNKS):
+        home(c).wait()
+        y_copy(c).wait_send()
+        for kind in range(Z_UP, KINDS):
+            sent(kind, c)
+            if kind >= X_UP:
+                got(kind, c)
+
+
+def halo_call(mesh, qkv, edge):
     frames, rows, cols, channels = qkv.shape
-    kv = qkv[..., channels // 3 :]
+    wide = edge.shape[-1]
+    sizes = {axis: mesh.shape[axis] for axis in ("ta", "ha", "hd")}
+    hbm = pl.BlockSpec(memory_space=pl.ANY)
+    return pl.pallas_call(
+        functools.partial(halo_kernel, sizes, channels - wide),
+        in_specs=[hbm, hbm],
+        out_specs=[hbm, hbm],
+        out_shape=[
+            jax.ShapeDtypeStruct((frames + 2 * TT, rows + 2 * TH, cols, wide), qkv.dtype),
+            jax.ShapeDtypeStruct((frames + 2 * TT, (rows + 2 * TH) * TW, wide), qkv.dtype),
+        ],
+        scratch_shapes=[
+            pltpu.SemaphoreType.DMA((KINDS, CHUNKS)),
+            pltpu.SemaphoreType.DMA((KINDS, CHUNKS)),
+            pltpu.SemaphoreType.DMA((CHUNKS,)),
+        ],
+        compiler_params=pltpu.CompilerParams(collective_id=0, has_side_effects=True),
+    )(qkv, edge)
+
+
+def column_shards(mesh, qkv, q_gain, k_gain, windows, frame_counts, row_counts):
+    frames, rows, cols, channels = qkv.shape
+    wide = channels // 3 * 2
     me = lax.axis_index("hd")
-    edge = lax.dynamic_slice_in_dim(kv, jnp.where(me == 0, cols - TW, 0), TW, axis=2)
-    side = lax.ppermute(edge, "hd", [(0, 1), (1, 0)])
-
-    def grown(value):
-        lo = shift(value[:, rows - TH :], "ha", 1)
-        hi = shift(value[:, :TH], "ha", -1)
-        value = jnp.concatenate([lo, value, hi], axis=1)
-        lo = shift(value[frames - TT :], "ta", 1)
-        hi = shift(value[:TT], "ta", -1)
-        return jnp.concatenate([lo, value, hi], axis=0)
-
-    ext = grown(kv)
-    side = grown(side).reshape(frames + 2 * TT, -1, kv.shape[-1])
+    zero = jnp.zeros((), jnp.int32)
+    edge = lax.dynamic_slice(
+        qkv, (zero, zero, jnp.where(me == 0, cols - TW, 0), zero + channels - wide), (frames, rows, TW, wide)
+    ).reshape(frames, rows * TW, wide)
+    ext, side = halo_call(mesh, qkv, edge)
     made = tables(frames, rows, cols, windows, frame_counts, row_counts)
     return attend_call(qkv, ext, side, *made, q_gain, k_gain)
 
 
 def solution(mesh):
     def shards(qkv, *rest):
-        fits = mesh.shape["hd"] == 2 and qkv.shape[2] % 16 == 0
-        return (column_shards if fits else head_shards)(qkv, *rest)
+        fits = mesh.shape["hd"] == 2 and min(mesh.shape["ta"], mesh.shape["ha"]) > 1 and qkv.shape[2] % 16 == 0
+        return column_shards(mesh, qkv, *rest) if fits else head_shards(qkv, *rest)
 
     return jax.shard_map(
         shards,

time: 268 us -> 621 us (2.32)
  the two profiles are of different devices: /device:TPU:1 before, /device:TPU:0 now
where the time goes in v2:
time: 621 us
  Pallas kernels  609 us (98%)
    pallas_call x1, Pallas kernels, halo_call(): pl.pallas_call(functools.partial(halo_kernel, sizes, channels - wide), in...  552 us
    pallas_call x1, Pallas kernels, attend_call(): pl.pallas_call(attend_kernel, grid_spec=grid_spec, out_shape=jax.ShapeDty...  57.3 us
  transfers between devices with their start and end apart: 1, of which 0 were waited for; matrix products, arithmetic and copies ran while one was open for 1% of the time, Pallas kernels for 89%

profile of v2, /device:TPU:0, one launch (start us, length us, event | category | flops | bytes accessed | tf_op | source)
XLA Modules:
  0.0 620.6 jit_solution(17452715504531732793)
XLA Ops:
  0.0 3.0 collective-permute-start
  3.0 0.1 iota_compare_fusion
  3.1 0.1 fusion.1
  3.2 0.8 select_reduce_fusion.1
  4.0 0.8 select_reduce_fusion
  4.9 0.1 slice_convert_fusion.1.flive
  5.0 0.1 and_not_fusion
  5.0 0.1 broadcast_and_fusion
  5.1 0.1 select_convert_fusion.1.kfy_ref
  5.2 0.2 select_convert_fusion.kfe_ref
  5.4 2.7 dynamic-slice_bitcast_fusion.edge
  8.1 0.0 copy-start.3
  8.1 0.0 copy-start.1
  8.1 0.0 copy-start.2
  8.1 0.1 slice_convert_fusion.rlive
  8.2 552.1 %shard_map.64 = (bf16[8,8,32,6144]{3,2,1,0:T(8,128)(2,1)}, bf16[8,64,6144]{2,1,0:T(8,128)(2,1)}) custom-call(bf16[4,4,32,9216]{3,2,1,0:T(8,128)(2,1)} %q_ref.1, bf16[4,32,6144]{2,1,0:T(8,128)(2,1)} %dynamic-slice_bitcast_fusion.edge), custom_call_target="tpu_custom_call" | custom-call | tf_op jit(solution)/shard_map/pallas_call | solution.py:406
  560.2 0.0 collective-permute-done
  560.3 0.0 copy-done.3
  560.3 0.1 pad_add_fusion.1
  560.3 0.1 copy.13
  560.4 0.1 copy.12
  560.5 0.0 copy-done.1
  560.5 0.0 copy-done.2
  560.6 0.0 copy-start
  560.6 2.8 copy-done
  563.3 57.3 %shard_map.65 = bf16[4,4,32,3072]{3,2,1,0:T(8,128)(2,1)} custom-call(s32[24,3]{1,0:T(8,128)S(1)} %broadcast_select_fusion.win, s32[4]{0:T(128)S(1)} %slice_convert_fusion.1.flive, s32[4]{0:T(128)S(1)} %slice_convert_fusion.rlive, bf16[4,4,32,9216]{3,2,1,0:T(8,128)(2,1)} %q_ref.1, bf16[8,8,32,6144]{3,2,1,0:T(8,128)(2,1)} %get-tuple-element.7.ke_ref.ve_ref, ...), custom_call_target="tpu_custom_call" | custom-call | flops 9059696640 | bytes 36175872 | tf_op jit(solution)/shard_map/pallas_call | solution.py:216
  (9 shorter events, 0.1 us)
Async XLA Ops:
  0.0 560.2 %collective-permute-start = (s32[12,3]{0,1:T(4,128)}, s32[12,3]{0,1:T(4,128)S(1)}, u32[]{:S(2)}, u32[]{:S(2)}) collective-permute-start(s32[12,3]{0,1:T(4,128)} %param.9), channel_id=1, source_target_pairs={{0,1},{1,0},{2,3},{3,2},{4,5},{5,4},{6,7},{7,6},{8,9},{9,8},{10,11... | collective-permute-start | bytes 440 | tf_op jit(solution)/shard_map/ppermute | solution.py:238
  8.1 552.2 %copy-start.3 = (s32[12,3]{0,1:T(4,128)S(1)}, s32[12,3]{0,1:T(4,128)}, u32[]{:S(2)}) copy-start(s32[12,3]{0,1:T(4,128)} %param.9) | copy-start | bytes 436
  8.1 552.5 %copy-start.1 = (f32[128]{0:T(128)S(1)}, f32[128]{0:T(128)}, u32[]{:S(2)}) copy-start(f32[128]{0:T(128)} %param.7) | copy-start | bytes 1540
  8.1 552.5 %copy-start.2 = (f32[128]{0:T(128)S(1)}, f32[128]{0:T(128)}, u32[]{:S(2)}) copy-start(f32[128]{0:T(128)} %param.8) | copy-start | bytes 1540
  560.6 2.8 copy-start

commit v3 on v2

--- a/solution.py
+++ b/solution.py
@@ -133,8 +133,8 @@
 
 
 def attend_kernel(
-    win, flive, rlive, q_ref, ke_ref, ve_ref, ky_ref, vy_ref, kfe_ref, kfy_ref, qf_ref,
-    qg_ref, kg_ref, o_ref, qn, kn, kyn,
+    win, flive, rlive, fin, rin, q_ref, k_ref, v_ref, ke_ref, ve_ref, ky_ref, vy_ref, kfe_ref, kfy_ref,
+    qf_ref, qg_ref, kg_ref, o_ref, qn, kn, kyn, vn, vyn,
 ):
     frames, rows, cols, dim = q_ref.shape
     halo = ky_ref.shape[1] // (rows + 2 * TH)
@@ -144,8 +144,18 @@
     for f in range(frames):
         qn[f] = unit_rms(q_ref[f], qg)
     for f in range(frames + 2 * TT):
-        kn[f] = unit_rms(ke_ref[f], kg)
-        kyn[f] = unit_rms(ky_ref[f], kg)
+        for r0, r1 in ((0, TH), (TH, TH + rows), (TH + rows, rows + 2 * TH)):
+            held = (fin[f] * rin[r0]) > 0
+            rs, ys = slice(r0, r1), slice(r0 * halo, r1 * halo)
+            there = lambda x: lax.select(held, x, jnp.zeros_like(x))
+            kyn[f, ys] = unit_rms(there(ky_ref[f, ys]), kg)
+            vyn[f, ys] = there(vy_ref[f, ys])
+            if TT <= f < frames + TT and r0 == TH:
+                kn[f, rs] = unit_rms(k_ref[f - TT], kg)
+                vn[f, rs] = v_ref[f - TT]
+            else:
+                kn[f, rs] = unit_rms(there(ke_ref[f, rs]), kg)
+                vn[f, rs] = there(ve_ref[f, rs])
     factor = math.log2(math.e) / math.sqrt(dim)
 
     def tile(t, r, near_t, near_r):
@@ -163,8 +173,8 @@
         p1 = jnp.exp2((s1 - top) * factor)
         p2 = jnp.exp2((s2 - top) * factor)
         summed = jnp.sum(p1, axis=1, keepdims=True) + jnp.sum(p2, axis=1, keepdims=True)
-        v1 = ve_ref[fs, rs].reshape(-1, dim)
-        v2 = vy_ref[fs, ys].reshape(-1, dim)
+        v1 = vn[fs, rs].reshape(-1, dim)
+        v2 = vyn[fs, ys].reshape(-1, dim)
         out = jnp.dot(p1.astype(jnp.bfloat16), v1, preferred_element_type=jnp.float32)
         out = out + jnp.dot(p2.astype(jnp.bfloat16), v2, preferred_element_type=jnp.float32)
         out = (out / summed).reshape(TT, TH, cols, dim)
@@ -184,7 +194,7 @@
                         tile(t, r, near_t, near_r)
 
 
-def attend_call(qkv, ext, side, win, flive, rlive, kfe, kfy, qf, q_gain, k_gain):
+def attend_call(qkv, ext, side, win, flive, rlive, fin, rin, kfe, kfy, qf, q_gain, k_gain):
     frames, rows, cols, channels = qkv.shape
     dim = q_gain.shape[0]
     heads = channels // (3 * dim)
@@ -192,10 +202,12 @@
     qg, kg = q_gain.reshape(1, dim), k_gain.reshape(1, dim)
     eb, yb = ext.shape[:3] + (dim,), side.shape[:2] + (dim,)
     grid_spec = pltpu.PrefetchScalarGridSpec(
-        num_scalar_prefetch=3,
+        num_scalar_prefetch=5,
         grid=(heads,),
         in_specs=[
             pl.BlockSpec((frames, rows, cols, dim), lambda h, *_: (0, 0, 0, h)),
+            pl.BlockSpec((frames, rows, cols, dim), lambda h, *_: (0, 0, 0, h + heads)),
+            pl.BlockSpec((frames, rows, cols, dim), lambda h, *_: (0, 0, 0, h + 2 * heads)),
             pl.BlockSpec(eb, lambda h, *_: (0, 0, 0, h)),
             pl.BlockSpec(eb, lambda h, *_: (0, 0, 0, h + heads)),
             pl.BlockSpec(yb, lambda h, *_: (0, 0, h)),
@@ -211,6 +223,8 @@
             pltpu.VMEM((frames, rows, cols, dim), jnp.bfloat16),
             pltpu.VMEM(eb, jnp.bfloat16),
             pltpu.VMEM(yb, jnp.bfloat16),
+            pltpu.VMEM(eb, jnp.bfloat16),
+            pltpu.VMEM(yb, jnp.bfloat16),
         ],
     )
     return pl.pallas_call(
@@ -223,7 +237,7 @@
             bytes_accessed=ext.size * 2 + side.size * 2 + qkv.size,
             transcendentals=heads * frames * rows * cols * 1440,
         ),
-    )(win, flive, rlive, qkv, ext, ext, side, side, kfe, kfy, qf, qg, kg)
+    )(win, flive, rlive, fin, rin, qkv, qkv, qkv, ext, ext, side, side, kfe, kfy, qf, qg, kg)
 
 
 def shift(value, axis, step):
@@ -258,7 +272,9 @@
     qf = jnp.where(far, MASKED, 0.0).astype(jnp.bfloat16)
     qf = jnp.broadcast_to(qf[:, None], (2, TT * TH, cols, FEATURES)).reshape(2, -1, FEATURES)
     count = lambda flags, width: flags.astype(jnp.int32)[width:-width]
-    return win, count(flive, TT), count(rlive, TH), kfe, kfy, qf
+    inside = lambda at, counts, extent: ((at >= 0) & (at < counts.shape[0] * extent)).astype(jnp.int32)
+    fin, rin = inside(at_f, frame_counts, TT), inside(at_r, row_counts, TH)
+    return win, count(flive, TT), count(rlive, TH), fin, rin, kfe, kfy, qf
 
 
 CHUNKS = 6
@@ -267,7 +283,7 @@
 KINDS = 13
 
 
-def halo_kernel(sizes, base, qkv, edge, ext, side, send_sem, recv_sem, own_sem):
+def halo_kernel(sizes, base, qkv, edge, ext, side, send_sem, recv_sem):
     frames, rows = qkv.shape[:2]
     f1, r1 = frames + TT, rows + TH
     width = ext.shape[-1] // CHUNKS
@@ -319,40 +335,37 @@
 
     def plan(kind, c):
         return {
-            Z_UP: ("ha", 1, own(OF, rlast, c), cells(F, RLO, c), own(OF, rfirst, c)),
-            Z_DOWN: ("ha", -1, own(OF, rfirst, c), cells(F, RHI, c), own(OF, rfirst, c)),
-            ZS_UP: ("ha", 1, strip(F, slice(rows, r1), c), strip(F, RLO, c), strip(OF, rfirst, c, edge)),
-            ZS_DOWN: ("ha", -1, strip(F, slice(TH, 2 * TH), c), strip(F, RHI, c), strip(OF, rfirst, c, edge)),
-            X_UP: ("ta", 1, own(last, slice(0, rows), c), cells(LO, R, c), own(first, slice(0, rows), c)),
-            X_DOWN: ("ta", -1, own(first, slice(0, rows), c), cells(HI, R, c), own(first, slice(0, rows), c)),
-            XLO_UP: ("ta", 1, cells(flast, RLO, c), cells(LO, RLO, c), own(first, rfirst, c)),
-            XLO_DOWN: ("ta", -1, cells(ffirst, RLO, c), cells(HI, RLO, c), own(first, rfirst, c)),
-            XHI_UP: ("ta", 1, cells(flast, RHI, c), cells(LO, RHI, c), own(first, rfirst, c)),
-            XHI_DOWN: ("ta", -1, cells(ffirst, RHI, c), cells(HI, RHI, c), own(first, rfirst, c)),
-            XS_UP: ("ta", 1, strip(flast, ROWS_ALL, c), strip(LO, ROWS_ALL, c), None),
-            XS_DOWN: ("ta", -1, strip(ffirst, ROWS_ALL, c), strip(HI, ROWS_ALL, c), None),
+            Z_UP: ("ha", 1, own(OF, rlast, c), cells(F, RLO, c)),
+            Z_DOWN: ("ha", -1, own(OF, rfirst, c), cells(F, RHI, c)),
+            ZS_UP: ("ha", 1, strip(F, slice(rows, r1), c), strip(F, RLO, c)),
+            ZS_DOWN: ("ha", -1, strip(F, slice(TH, 2 * TH), c), strip(F, RHI, c)),
+            X_UP: ("ta", 1, own(last, slice(0, rows), c), cells(LO, R, c)),
+            X_DOWN: ("ta", -1, own(first, slice(0, rows), c), cells(HI, R, c)),
+            XLO_UP: ("ta", 1, cells(flast, RLO, c), cells(LO, RLO, c)),
+            XLO_DOWN: ("ta", -1, cells(ffirst, RLO, c), cells(HI, RLO, c)),
+            XHI_UP: ("ta", 1, cells(flast, RHI, c), cells(LO, RHI, c)),
+            XHI_DOWN: ("ta", -1, cells(ffirst, RHI, c), cells(HI, RHI, c)),
+            XS_UP: ("ta", 1, strip(flast, ROWS_ALL, c), strip(LO, ROWS_ALL, c)),
+            XS_DOWN: ("ta", -1, strip(ffirst, ROWS_ALL, c), strip(HI, ROWS_ALL, c)),
         }[kind]
 
     def start(kind, c):
-        axis, step, src, dst, fill = plan(kind, c)
-        if fill is None:
-            fill = strip(ffirst, ROWS_ALL, c)
-        sends, gets = (up, down) if step == 1 else (down, up)
+        axis, step, src, dst = plan(kind, c)
+        sends = up if step == 1 else down
 
         @pl.when(sends[axis])
         def _():
             remote(kind, c, src, dst, {axis: at[axis] + step}).start()
 
-        @pl.when(jnp.logical_not(gets[axis]))
+    def got(kind, c):
+        axis, step, _, dst = plan(kind, c)
+
+        @pl.when((down if step == 1 else up)[axis])
         def _():
-            pltpu.make_async_copy(fill, dst, recv_sem.at[kind, c]).start()
-
-    def got(kind, c):
-        dst = plan(kind, c)[3]
-        pltpu.make_async_copy(dst, dst, recv_sem.at[kind, c]).wait()
+            pltpu.make_async_copy(dst, dst, recv_sem.at[kind, c]).wait()
 
     def sent(kind, c):
-        axis, step, src, dst, _ = plan(kind, c)
+        axis, step, src, dst = plan(kind, c)
 
         @pl.when((up if step == 1 else down)[axis])
         def _():
@@ -360,9 +373,6 @@
 
     def y_copy(c):
         return remote(Y_OWN, c, strip(OF, slice(0, rows), c, edge), strip(F, R, c), partner)
-
-    def home(c):
-        return pltpu.make_async_copy(own(OF, slice(0, rows), c), cells(F, R, c), own_sem.at[c])
 
     ahead = 2
     for c in range(CHUNKS):
@@ -371,7 +381,6 @@
         if c < CHUNKS:
             for kind in (Z_UP, Z_DOWN, X_UP, X_DOWN):
                 start(kind, c)
-            home(c).start()
         d = c - 1
         if 0 <= d < CHUNKS:
             y_copy(d).wait_recv()
@@ -390,7 +399,6 @@
             start(XS_UP, e)
             start(XS_DOWN, e)
     for c in range(CHUNKS):
-        home(c).wait()
         y_copy(c).wait_send()
         for kind in range(Z_UP, KINDS):
             sent(kind, c)
@@ -414,7 +422,6 @@
         scratch_shapes=[
             pltpu.SemaphoreType.DMA((KINDS, CHUNKS)),
             pltpu.SemaphoreType.DMA((KINDS, CHUNKS)),
-            pltpu.SemaphoreType.DMA((CHUNKS,)),
         ],
         compiler_params=pltpu.CompilerParams(collective_id=0, has_side_effects=True),
     )(qkv, edge)

time: 621 us -> 171 us (0.28)
  the two profiles are of different devices: /device:TPU:0 before, /device:TPU:1 now
where the time goes in v3:
time: 171 us; the launch traced here: 174 us
  Pallas kernels  163 us (95%)
  local copies, waits for them, and re-layouts  5.67 us (3%)
  other arithmetic  2.52 us (1%)
  starting transfers between devices  2.07 us (1%)
    pallas_call x1, Pallas kernels, halo_call(): pl.pallas_call(functools.partial(halo_kernel, sizes, channels - wide), in...  103 us
    pallas_call x1, Pallas kernels, attend_call(): pl.pallas_call(attend_kernel, grid_spec=grid_spec, out_shape=jax.ShapeDty...  60.4 us
  transfers between devices with their start and end apart: 1, of which 0 were waited for; matrix products, arithmetic and copies ran while one was open for 3% of the time, Pallas kernels for 59%

profile of v3, /device:TPU:1, one launch (start us, length us, event | category | flops | bytes accessed | tf_op | source)
XLA Modules:
  0.0 173.5 jit_solution(16881216106132675548)
XLA Ops:
  0.0 2.1 %collective-permute-start = (s32[12,3]{0,1:T(4,128)}, s32[12,3]{0,1:T(4,128)S(1)}, u32[]{:S(2)}, u32[]{:S(2)}) collective-permute-start(s32[12,3]{0,1:T(4,128)} %param.9), channel_id=1, source_target_pairs={{0,1},{1,0},{2,3},{3,2},{4,5},{5,4},{6,7},{7,6},{8,9},{9,8},{10,11... | collective-permute-start | bytes 440 | tf_op jit(solution)/shard_map/ppermute | solution.py:252
  2.1 0.1 iota_compare_fusion
  2.2 0.1 fusion.1
  2.3 0.8 select_reduce_fusion.1
  3.1 0.1 slice_convert_fusion.1.flive
  3.2 0.8 select_reduce_fusion
  4.1 0.1 and_not_fusion
  4.2 0.1 broadcast_and_fusion
  4.2 0.1 select_convert_fusion.1.kfy_ref
  4.3 0.2 select_convert_fusion.kfe_ref
  4.5 2.7 %dynamic-slice_bitcast_fusion.edge = bf16[4,32,6144]{2,1,0:T(8,128)(2,1)} fusion(bf16[4,4,32,9216]{3,2,1,0:T(8,128)(2,1)} %v_ref.1, s32[]{:T(128)S(6)} %select_n.92), kind=kLoop, calls=%fused_computation | loop fusion | bytes 3145732 | tf_op jit(solution)/shard_map/reshape | solution.py:437
  7.2 0.0 copy-start.3
  7.2 0.0 copy-start.1
  7.2 0.0 copy-start.2
  7.2 0.1 slice_convert_fusion.rlive
  7.3 102.7 %shard_map.64 = (bf16[8,8,32,6144]{3,2,1,0:T(8,128)(2,1)}, bf16[8,64,6144]{2,1,0:T(8,128)(2,1)}) custom-call(bf16[4,4,32,9216]{3,2,1,0:T(8,128)(2,1)} %v_ref.1, bf16[4,32,6144]{2,1,0:T(8,128)(2,1)} %dynamic-slice_bitcast_fusion.edge), custom_call_target="tpu_custom_call" | custom-call | tf_op jit(solution)/shard_map/pallas_call | solution.py:414
  110.0 0.0 collective-permute-done
  110.0 0.0 copy-done.3
  110.0 0.1 pad_add_fusion.1
  110.1 0.1 copy.13
  110.2 0.1 copy.12
  110.3 0.0 copy-done.1
  110.3 0.0 copy-done.2
  110.3 0.0 copy-start
  110.3 2.8 %copy-done = bf16[8,64,6144]{2,1,0:T(8,128)(2,1)S(1)} copy-done((bf16[8,64,6144]{2,1,0:T(8,128)(2,1)S(1)}, bf16[8,64,6144]{2,1,0:T(8,128)(2,1)}, u32[]{:S(2)}) %copy-start) | copy-done | bytes 6291480
  113.1 60.4 %shard_map.65 = bf16[4,4,32,3072]{3,2,1,0:T(8,128)(2,1)} custom-call(s32[24,3]{1,0:T(8,128)S(1)} %broadcast_select_fusion.win, s32[4]{0:T(128)S(1)} %slice_convert_fusion.1.flive, s32[4]{0:T(128)S(1)} %slice_convert_fusion.rlive, s32[8]{0:T(128)S(1)} %get-tuple-element.13.fin, s32[8]{0:T(128)S(1)} %get-tuple-element.15.rin, bf16[4,4,32,9216]{3,2,1,0:T(8,128)(2,1)} %v_ref.1, ...), custom_call_target="tpu_custom_call" | custom-call | flops 9059696640 | bytes 36175872 | tf_op jit(solution)/shard_map/pallas_call | solution.py:230
  (10 shorter events, 0.1 us)
Async XLA Ops:
  0.0 110.0 %collective-permute-start = (s32[12,3]{0,1:T(4,128)}, s32[12,3]{0,1:T(4,128)S(1)}, u32[]{:S(2)}, u32[]{:S(2)}) collective-permute-start(s32[12,3]{0,1:T(4,128)} %param.9), channel_id=1, source_target_pairs={{0,1},{1,0},{2,3},{3,2},{4,5},{5,4},{6,7},{7,6},{8,9},{9,8},{10,11... | collective-permute-start | bytes 440 | tf_op jit(solution)/shard_map/ppermute | solution.py:252
  7.2 102.8 %copy-start.3 = (s32[12,3]{0,1:T(4,128)S(1)}, s32[12,3]{0,1:T(4,128)}, u32[]{:S(2)}) copy-start(s32[12,3]{0,1:T(4,128)} %param.9) | copy-start | bytes 436
  7.2 103.1 %copy-start.1 = (f32[128]{0:T(128)S(1)}, f32[128]{0:T(128)}, u32[]{:S(2)}) copy-start(f32[128]{0:T(128)} %param.7) | copy-start | bytes 1540
  7.2 103.1 %copy-start.2 = (f32[128]{0:T(128)S(1)}, f32[128]{0:T(128)}, u32[]{:S(2)}) copy-start(f32[128]{0:T(128)} %param.8) | copy-start | bytes 1540
  110.3 2.8 %copy-start = (bf16[8,64,6144]{2,1,0:T(8,128)(2,1)S(1)}, bf16[8,64,6144]{2,1,0:T(8,128)(2,1)}, u32[]{:S(2)}) copy-start(bf16[8,64,6144]{2,1,0:T(8,128)(2,1)} %get-tuple-element.8.ky_ref.vy_ref) | copy-start | bytes 18874372
